TPU v7x, 32 devices: a whole 2x2x4 slice. The times are simulated.
32 devices in a mesh: events: 4 (over z), nodes: 8 (over y, x, core).
Axes of the slice: x: 2, y: 2, z: 4, core: 2. Of those that a mesh axis runs over, the one named last changes fastest.
Arguments:
- nodes_in: bfloat16 [4, 16384, 128], P('events', 'nodes'), may hold values from -6 to 6
- edge_latents: bfloat16 [4, 8, 8, 2, 128, 128], P('events', 'nodes'), may hold values from -6 to 6
- src_block: int32 [4, 8, 8, 2], P('events', 'nodes'), may hold values from 0 to 15
- src_offset: int32 [4, 8, 8, 2, 128], P('events', 'nodes'), may hold values from 0 to 127
- dst_block: int32 [4, 8, 8, 2], P('events', 'nodes'), may hold values from 0 to 15
- dst_offset: int32 [4, 8, 8, 2, 128], P('events', 'nodes'), may hold values from 0 to 127
- tile_counts: int32 [4, 8, 8], P('events'), may hold values from 1 to 2, as said below
- w_edge1: bfloat16 [384, 128], replicated, may hold values from -0.3125 to 0.3125
- b_edge1: float32 [128], replicated, may hold values from -3 to 3
- w_edge2: bfloat16 [128, 128], replicated, may hold values from -0.5 to 0.5
- b_edge2: float32 [128], replicated, may hold values from -3 to 3
- w_node1: bfloat16 [256, 128], replicated, may hold values from -0.375 to 0.375
- b_node1: float32 [128], replicated, may hold values from -3 to 3
- w_node2: bfloat16 [128, 128], replicated, may hold values from -0.5 to 0.5
- b_node2: float32 [128], replicated, may hold values from -3 to 3
- cotangent: bfloat16 [4, 16384, 128], P('events', 'nodes'), may hold values from -6 to 6
Outputs:
- new_nodes: bfloat16 [4, 16384, 128], P('events', 'nodes')
- node_grads: bfloat16 [4, 16384, 128], P('events', 'nodes')
- grad_w_edge1: float32 [384, 128], replicated
- grad_b_edge1: float32 [128], replicated
- grad_w_edge2: float32 [128, 128], replicated
- grad_b_edge2: float32 [128], replicated
- grad_w_node1: float32 [256, 128], replicated
- grad_b_node1: float32 [128], replicated
- grad_w_node2: float32 [128, 128], replicated
- grad_b_node2: float32 [128], replicated
Inputs may be any that keep to these rules, and one draw needn't show every extreme that they name: tile_counts[g, s, d] is the number of live slots from source device s to destination device d; in every event group some destination device receives exactly 2 tiles from every source device.
All inputs are finite; a program needn't handle non-finite values.
Results may differ from a plain program's by a relative error of at most 0.0067.
Values may be sent and summed in bfloat16 or wider, within the bound.
A program may use at most 64 MiB of HBM per device.

v0:
```python
import jax
import jax.numpy as jnp
from jax import lax
from jax.sharding import PartitionSpec as P


def silu_slope(value):
    sig = jax.nn.sigmoid(value)
    return sig * (1.0 + value * (1.0 - sig))


def tile_onehot(offsets, tile):
    return (offsets[..., None] == jnp.arange(tile, dtype=jnp.int32)[None, None, :]).astype(
        jnp.bfloat16
    )


def gather_tiles(table, blocks, onehot):
    tile = onehot.shape[-1]
    picked = table.reshape(-1, tile, table.shape[-1])[blocks]
    return jnp.einsum("ten,tnd->ted", onehot, picked, preferred_element_type=jnp.float32).astype(
        table.dtype
    )


def scatter_tiles(values, blocks, onehot, block_count):
    if values.dtype == jnp.bfloat16:
        per_tile = jnp.einsum("ten,ted->tnd", onehot, values, preferred_element_type=jnp.float32)
    else:
        per_tile = jnp.einsum(
            "ten,ted->tnd", onehot.astype(jnp.float32), values, precision=lax.Precision.HIGHEST
        )
    picker = (blocks[:, None] == jnp.arange(block_count, dtype=jnp.int32)[None, :]).astype(
        jnp.float32
    )
    summed = jnp.einsum("tb,tnd->bnd", picker, per_tile, precision=lax.Precision.HIGHEST)
    return summed.reshape(-1, values.shape[-1])


def shards(
    nodes_in,
    edge_latents,
    src_block,
    src_offset,
    dst_block,
    dst_offset,
    tile_counts,
    w_edge1,
    b_edge1,
    w_edge2,
    b_edge2,
    w_node1,
    b_node1,
    w_node2,
    b_node2,
    cotangent,
):
    peers = lax.axis_size("nodes")
    myself = lax.axis_index("nodes")
    nodes = nodes_in[0]
    cot = cotangent[0]
    node_rows, width = nodes.shape
    tile = src_offset.shape[-1]
    slots = src_offset.shape[3]
    block_count = node_rows // tile
    tiles_all = peers * slots
    scale_factor = float(lax.axis_size("events") * peers * node_rows) ** (-0.5)
    w_src, w_dst, w_lat = (w_edge1[:width], w_edge1[width : 2 * width], w_edge1[2 * width :])
    w_own, w_agg = (w_node1[:width], w_node1[width:])
    send_blocks = src_block[0, 0].reshape(-1)
    send_hot = tile_onehot(src_offset[0, 0].reshape(tiles_all, tile), tile)
    recv_blocks = dst_block[0, 0].reshape(-1)
    recv_hot = tile_onehot(dst_offset[0, 0].reshape(tiles_all, tile), tile)
    outgoing = gather_tiles(nodes, send_blocks, send_hot).reshape(peers, slots, tile, width)
    h_src = lax.all_to_all(outgoing, "nodes", split_axis=0, concat_axis=0, tiled=True).reshape(
        -1, width
    )
    counts = lax.dynamic_index_in_dim(tile_counts[0], myself, 1, keepdims=False)
    live = jnp.arange(slots, dtype=jnp.int32)[None, :] < counts[:, None]
    live = (
        jnp.broadcast_to(live[..., None], (peers, slots, tile)).reshape(-1, 1).astype(jnp.bfloat16)
    )
    lat = edge_latents[0, 0].reshape(-1, width)
    h_dst = gather_tiles(nodes, recv_blocks, recv_hot).reshape(-1, width)
    z_one = (
        jnp.dot(h_src, w_src, preferred_element_type=jnp.float32)
        + jnp.dot(h_dst, w_dst, preferred_element_type=jnp.float32)
        + jnp.dot(lat, w_lat, preferred_element_type=jnp.float32)
        + b_edge1
    )
    a_one = jax.nn.silu(z_one).astype(jnp.bfloat16)
    message = (jnp.dot(a_one, w_edge2, preferred_element_type=jnp.float32) + b_edge2).astype(
        jnp.bfloat16
    ) * live
    agg = scatter_tiles(
        message.reshape(tiles_all, tile, width), recv_blocks, recv_hot, block_count
    ).astype(jnp.bfloat16)
    z_two = (
        jnp.dot(nodes, w_own, preferred_element_type=jnp.float32)
        + jnp.dot(agg, w_agg, preferred_element_type=jnp.float32)
        + b_node1
    )
    a_two = jax.nn.silu(z_two).astype(jnp.bfloat16)
    updated = (
        nodes.astype(jnp.float32)
        + jnp.dot(a_two, w_node2, preferred_element_type=jnp.float32)
        + b_node2
    ).astype(jnp.bfloat16)
    g_two = (
        jnp.dot(cot, w_node2.T, preferred_element_type=jnp.float32) * silu_slope(z_two)
    ).astype(jnp.bfloat16)
    node_terms = (
        jnp.concatenate(
            [
                jnp.dot(nodes.T, g_two, preferred_element_type=jnp.float32),
                jnp.dot(agg.T, g_two, preferred_element_type=jnp.float32),
            ],
            axis=0,
        ),
        jnp.sum(g_two.astype(jnp.float32), axis=0),
        jnp.dot(a_two.T, cot, preferred_element_type=jnp.float32),
        jnp.sum(cot.astype(jnp.float32), axis=0),
    )
    g_agg = jnp.dot(g_two, w_agg.T, preferred_element_type=jnp.float32).astype(jnp.bfloat16)
    g_msg = gather_tiles(g_agg, recv_blocks, recv_hot).reshape(-1, width) * live
    g_one = (
        jnp.dot(g_msg, w_edge2.T, preferred_element_type=jnp.float32) * silu_slope(z_one)
    ).astype(jnp.bfloat16)
    g_src = jnp.dot(g_one, w_src.T, preferred_element_type=jnp.float32).reshape(
        peers, slots, tile, width
    )
    returned = (
        lax.all_to_all(g_src.astype(jnp.bfloat16), "nodes", split_axis=0, concat_axis=0, tiled=True)
        .astype(g_src.dtype)
        .reshape(-1, width)
    )
    g_dst = jnp.dot(g_one, w_dst.T, preferred_element_type=jnp.float32)
    total = cot.astype(jnp.float32) + jnp.dot(g_two, w_own.T, preferred_element_type=jnp.float32)
    total = total + scatter_tiles(
        g_dst.reshape(tiles_all, tile, width), recv_blocks, recv_hot, block_count
    )
    total = total + scatter_tiles(
        returned.reshape(tiles_all, tile, width), send_blocks, send_hot, block_count
    )
    edge_terms = (
        jnp.concatenate(
            [
                jnp.dot(h_src.T, g_one, preferred_element_type=jnp.float32),
                jnp.dot(h_dst.T, g_one, preferred_element_type=jnp.float32),
                jnp.dot(lat.T, g_one, preferred_element_type=jnp.float32),
            ],
            axis=0,
        ),
        jnp.sum(g_one.astype(jnp.float32), axis=0),
        jnp.dot(a_one.T, g_msg, preferred_element_type=jnp.float32),
        jnp.sum(g_msg.astype(jnp.float32), axis=0),
    )
    summed = lax.psum(
        (
            edge_terms[0],
            edge_terms[1],
            edge_terms[2],
            edge_terms[3],
            node_terms[0],
            node_terms[1],
            node_terms[2],
            node_terms[3],
        ),
        ("events", "nodes"),
    )
    scaled = [value * scale_factor for value in summed]
    return (
        updated[None],
        total.astype(jnp.bfloat16)[None],
        scaled[0],
        scaled[1],
        scaled[2],
        scaled[3],
        scaled[4],
        scaled[5],
        scaled[6],
        scaled[7],
    )


def solution(mesh):
    return jax.shard_map(
        shards,
        mesh=mesh,
        in_specs=(
            P("events", "nodes", None),
            P("events", "nodes", None, None, None, None),
            P("events", "nodes", None, None),
            P("events", "nodes", None, None, None),
            P("events", "nodes", None, None),
            P("events", "nodes", None, None, None),
            P("events", None, None),
            P(),
            P(),
            P(),
            P(),
            P(),
            P(),
            P(),
            P(),
            P("events", "nodes", None),
        ),
        out_specs=(
            P("events", "nodes", None),
            P("events", "nodes", None),
            P(),
            P(),
            P(),
            P(),
            P(),
            P(),
            P(),
            P(),
        ),
        check_vma=False,
    )
```

profile of v0, /device:TPU:1, one launch (start us, length us, event | category | flops | bytes accessed | tf_op | source)
XLA Modules:
  0.0 243.8 jit_solution(3081769146235548526)
XLA Ops:
  7.2 0.8 copy.33
  8.1 1.7 gather_fusion
  9.8 1.3 convolution_convert_fusion.4
  11.1 5.4 %all-to-all-start = ((bf16[8,2,128,128]{3,2,1,0:T(8,128)(2,1)}), bf16[8,2,128,128]{3,2,1,0:T(8,128)(2,1)S(1)}, u32[]{:S(2)}, u32[]{:S(2)}) async-start(bf16[8,2,128,128]{3,2,1,0:T(8,128)(2,1)} %bitcast.6), calls=%async_computation | async-start | bytes 1048576 | tf_op jit(solution)/shard_map/all_to_all | solution.py:75
  20.1 0.9 convert_reduce_fusion
  20.9 1.2 fusion.25
  22.2 1.0 all-to-all-done
  24.4 1.4 multiply_convert_fusion.1
  27.0 1.0 fusion.20
  28.0 1.2 convolution_convert_fusion.5
  30.0 1.3 multiply_convert_fusion
  31.3 1.0 convert_reduce_fusion.1
  33.0 1.1 convolution_convert_fusion.1
  34.1 2.5 %gather_fusion.2 = bf16[16,128,128]{2,1,0:T(8,128)(2,1)} fusion(bf16[16,128,128]{2,1,0:T(8,128)(2,1)} %bitcast.107, s32[1024]{0:T(1024)S(1)} %pad_clamp_fusion), kind=kCustom, calls=%fused_computation.2 | custom fusion | bytes 1048640 | tf_op jit(solution)/shard_map/gather | solution.py:20
  36.5 2.3 convert_reduce_fusion.2
  39.1 0.7 copy-done.6
  39.8 1.0 fusion.57
  40.8 1.0 convert_reduce_fusion.3
  43.4 1.1 convolution_convert_fusion
  44.8 0.7 copy-done.3
  45.5 1.0 fusion.21
  46.5 1.1 fusion.11
  47.6 7.0 %all-to-all-start.1 = ((bf16[8,2,128,128]{3,2,1,0:T(8,128)(2,1)}), bf16[8,2,128,128]{3,2,1,0:T(8,128)(2,1)}, u32[]{:S(2)}, u32[]{:S(2)}) async-start(bf16[8,2,128,128]{3,2,1,0:T(8,128)(2,1)} %bitcast.104), calls=%async_computation.1 | async-start | bytes 1048576 | tf_op jit(solution)/shard_map/all_to_all | solution.py:133
  54.6 1.5 fusion.19
  56.2 2.2 fusion.15
  60.4 39.4 %all-reduce = (f32[128]{0:T(128)S(1)}, f32[128]{0:T(128)S(1)}, f32[128]{0:T(128)S(1)}, f32[128]{0:T(128)S(1)}) all-reduce(f32[128]{0:T(128)S(1)} %copy-done.26, f32[128]{0:T(128)S(1)} %copy-done.25, f32[128]{0:T(128)S(1)} %copy-done.24, f32[128]{0:T(128)S(1)} %copy-done.21), channel_id=1, replica_groups=mesh['events'=4,'nodes'=8] {'events','nodes'}, use_global_device_ids=true, to_apply=%region_2.3 | all-reduce | flops 512 | bytes 4096 | tf_op jit(solution)/shard_map/psum | solution.py:158
  100.4 1.6 copy.36
  102.5 126.7 %all-reduce.4.cloned.1.call-done = (f32[384,128]{1,0:T(8,128)}, f32[128,128]{1,0:T(8,128)}, f32[256,128]{1,0:T(8,128)}, f32[128,128]{1,0:T(8,128)}) async-done(((f32[384,128]{1,0:T(8,128)}, f32[128,128]{1,0:T(8,128)}, f32[256,128]{1,0:T(8,128)}, f32[128,128]{1,0:T(8,128)}), (f32[384,128]{1,0:T(8,128)}, f32[128,128]{1,0:T(8,128)}, f32[256,128]{1,0:T(8,128)}, ...) | async-done | bytes 458768 | tf_op jit(solution)/shard_map/psum | solution.py:158
  229.2 1.6 broadcast_multiply_fusion.1
  232.5 1.8 fusion.18
  234.2 1.2 fusion.13
  235.8 1.1 fusion.10
  (98 shorter events, 14.8 us)
Async XLA Ops:
  7.2 16.6 %copy-start = (bf16[1,1,8,2,128,128]{5,4,3,2,1,0:T(8,128)(2,1)S(1)}, bf16[1,1,8,2,128,128]{5,4,3,2,1,0:T(8,128)(2,1)}, u32[]{:S(2)}) copy-start(bf16[1,1,8,2,128,128]{5,4,3,2,1,0:T(8,128)(2,1)} %param.17) | copy-start | bytes 1572868
  8.1 1.7 copy-start.14
  11.1 6.2 %copy-start.1 = (bf16[1,2048,128]{2,1,0:T(8,128)(2,1)S(1)}, bf16[1,2048,128]{2,1,0:T(8,128)(2,1)}, u32[]{:S(2)}) copy-start(bf16[1,2048,128]{2,1,0:T(8,128)(2,1)} %param.16) | copy-start | bytes 1572868
  11.1 12.1 %all-to-all-start = ((bf16[8,2,128,128]{3,2,1,0:T(8,128)(2,1)}), bf16[8,2,128,128]{3,2,1,0:T(8,128)(2,1)S(1)}, u32[]{:S(2)}, u32[]{:S(2)}) async-start(bf16[8,2,128,128]{3,2,1,0:T(8,128)(2,1)} %bitcast.6), calls=%async_computation | async-start | bytes 1048576 | tf_op jit(solution)/shard_map/all_to_all | solution.py:75
  16.4 0.7 copy-start.22
  17.3 0.7 copy-start.19
  18.0 0.7 copy-start.11
  18.7 1.4 copy-start.2
  20.0 8.0 %copy-start.17 = (s32[16]{0:T(128)}, s32[16]{0:T(128)S(1)}, u32[]{:S(2)}) copy-start(s32[16]{0:T(128)S(1)} %eq.32) | copy-start | bytes 196
  20.0 0.9 copy-start.10
  20.9 2.2 copy-start.8
  24.4 1.5 copy-start.27
  25.8 1.1 copy-start.5
  25.9 0.7 copy-start.29
  28.0 1.4 copy-start.4
  30.0 1.3 copy-start.15
  38.8 1.0 copy-start.6
  38.8 2.0 copy-start.31
  42.5 0.9 copy-start.9
  44.5 1.0 copy-start.3
  45.5 1.0 copy-start.16
  45.5 1.0 copy-start.23
  47.6 184.8 %all-to-all-start.1 = ((bf16[8,2,128,128]{3,2,1,0:T(8,128)(2,1)}), bf16[8,2,128,128]{3,2,1,0:T(8,128)(2,1)}, u32[]{:S(2)}, u32[]{:S(2)}) async-start(bf16[8,2,128,128]{3,2,1,0:T(8,128)(2,1)} %bitcast.104), calls=%async_computation.1 | async-start | bytes 1048576 | tf_op jit(solution)/shard_map/all_to_all | solution.py:133
  54.6 174.6 %all-reduce.4.cloned.1.call-start = ((), (), s32[]{:S(2)}) async-start(), calls=%async_computation.2 | async-start | bytes 917504 | tf_op jit(solution)/shard_map/psum | solution.py:158
  54.6 1.5 copy-start.18
  59.0 0.7 copy-start.26
  59.7 0.7 copy-start.24
  59.7 0.7 copy-start.25
  229.2 1.6 copy-start.12
  229.2 1.6 copy-start.13
  230.8 1.0 copy-start.7
  232.4 1.8 copy-start.20
  (3 other events, 2.0 us)
Sparse Core Ops, SparseCore 0:
  100.0 129.1 all-reduce.3
where the time goes:
time: 245 us; the launch traced here: 244 us
  waiting for transfers between devices  128 us (52%)
  blocking collectives  39.4 us (16%)
  matrix products  28.1 us (11%)
  local copies, waits for them, and re-layouts  15.2 us (6%)
  between operations  14.3 us (6%)
  starting transfers between devices  12.4 us (5%)
  other arithmetic  6.65 us (3%)
    psum x1, waiting for transfers between devices, shards(): lax.psum((edge_terms[0], edge_terms[1], edge_terms[2], edge_terms[3], nod...  127 us
    psum x1, blocking collectives, shards(): lax.psum((edge_terms[0], edge_terms[1], edge_terms[2], edge_terms[3], nod...  39.4 us
    unnamed x66, local copies, waits for them, and re-layouts  7.1 us
    all_to_all x1, starting transfers between devices, shards(): lax.all_to_all(g_src.astype(jnp.bfloat16), 'nodes', split_axis=0, concat_...  7.01 us
    all_to_all x1, starting transfers between devices, shards(): lax.all_to_all(outgoing, 'nodes', split_axis=0, concat_axis=0, tiled=True)  5.35 us
  transfers between devices with their start and end apart: 3, of which 2 were waited for; matrix products, arithmetic and copies ran while one was open for 6% of the time, Pallas kernels for 0%

commit v1 on v0

--- a/solution.py
+++ b/solution.py
@@ -1,7 +1,30 @@
+import functools
 import jax
 import jax.numpy as jnp
 from jax import lax
 from jax.sharding import PartitionSpec as P
+
+
+def trace_vectors(q_in, comm_axis):
+    right_arr = lax.psum(1, axis_name=comm_axis)
+    current_arr = lax.axis_index(comm_axis)
+    left_arr, res = (right_arr, current_arr)
+    view_out = q_in.shape[0] // left_arr
+    e_next = jnp.roll(q_in, -res * view_out, 0)
+    local_now = lax.slice_in_dim(e_next, 0, view_out, axis=0)
+    steps_seen = [local_now]
+    for rr in range(1, left_arr):
+        mat_out = lax.slice_in_dim(e_next, rr * view_out, (rr + 1) * view_out, axis=0)
+        local_out = lax.ppermute(
+            mat_out, axis_name=comm_axis, perm=[(c, (c + rr) % left_arr) for c in range(left_arr)]
+        )
+        steps_seen.append(local_out)
+    found_now = jnp.concatenate(steps_seen[::-1], 0)
+    arr_out = jnp.roll(found_now, (res + 1) * steps_seen[0].shape[0], 0)
+    return arr_out
+
+
+leaves_make = functools.partial(trace_vectors, comm_axis="nodes")
 
 
 def silu_slope(value):
@@ -129,11 +152,7 @@
     g_src = jnp.dot(g_one, w_src.T, preferred_element_type=jnp.float32).reshape(
         peers, slots, tile, width
     )
-    returned = (
-        lax.all_to_all(g_src.astype(jnp.bfloat16), "nodes", split_axis=0, concat_axis=0, tiled=True)
-        .astype(g_src.dtype)
-        .reshape(-1, width)
-    )
+    returned = leaves_make(g_src.astype(jnp.bfloat16)).astype(g_src.dtype).reshape(-1, width)
     g_dst = jnp.dot(g_one, w_dst.T, preferred_element_type=jnp.float32)
     total = cot.astype(jnp.float32) + jnp.dot(g_two, w_own.T, preferred_element_type=jnp.float32)
     total = total + scatter_tiles(

time: 245 us -> 244 us (level)
  waiting for transfers between devices: 128 us -> 117 us
  local copies, waits for them, and re-layouts: 15.2 us -> 19.4 us
  other arithmetic: 6.65 us -> 9.63 us
  starting transfers between devices: 12.4 us -> 14.9 us
    psum x1, waiting for transfers between devices: 127 us -> 111 us  [shards(): lax.psum((edge_terms[0], edge_terms[1], edge_terms[2], edge_terms[3], nod...]
    ppermute x0 -> x7, starting transfers between devices: none -> 9.55 us  [trace_vectors(): lax.ppermute(mat_out, axis_name=comm_axis, perm=[(c, (c + rr) % left_arr)...]
    all_to_all x1 -> x0, starting transfers between devices: 7.01 us -> none  [shards(): lax.all_to_all(g_src.astype(jnp.bfloat16), 'nodes', split_axis=0, concat_...]
    unnamed x66 -> x75, local copies, waits for them, and re-layouts: 7.1 us -> 11.9 us
    ppermute x0 -> x7, waiting for transfers between devices: none -> 4.01 us  [trace_vectors(): lax.ppermute(mat_out, axis_name=comm_axis, perm=[(c, (c + rr) % left_arr)...]
    mul x5 -> x8, other arithmetic: 3.99 us -> 5.64 us  [shards(): scaled = [value * scale_factor for value in summed]]
  transfers between devices with their start and end apart: 3 -> 9, of which waited for: 2 -> 4; matrix products, arithmetic and copies ran while one was open for 6% -> 7% of each run, Pallas kernels for 0% -> 0%
where the time goes in v1:
time: 244 us; the launch traced here: 243 us
  waiting for transfers between devices  117 us (48%)
  blocking collectives  41.2 us (17%)
  matrix products  26.2 us (11%)
  local copies, waits for them, and re-layouts  19.4 us (8%)
  starting transfers between devices  14.9 us (6%)
  between operations  14.4 us (6%)
  other arithmetic  9.63 us (4%)
    psum x1, waiting for transfers between devices, shards(): lax.psum((edge_terms[0], edge_terms[1], edge_terms[2], edge_terms[3], nod...  111 us
    psum x1, blocking collectives, shards(): lax.psum((edge_terms[0], edge_terms[1], edge_terms[2], edge_terms[3], nod...  41.2 us
    unnamed x75, local copies, waits for them, and re-layouts  11.9 us
    ppermute x7, starting transfers between devices, trace_vectors(): lax.ppermute(mat_out, axis_name=comm_axis, perm=[(c, (c + rr) % left_arr)...  9.55 us
    mul x8, other arithmetic, shards(): scaled = [value * scale_factor for value in summed]  5.64 us
    all_to_all x1, starting transfers between devices, shards(): lax.all_to_all(outgoing, 'nodes', split_axis=0, concat_axis=0, tiled=True)  5.35 us
  transfers between devices with their start and end apart: 9, of which 4 were waited for; matrix products, arithmetic and copies ran while one was open for 7% of the time, Pallas kernels for 0%

profile of v1, /device:TPU:1, one launch (start us, length us, event | category | flops | bytes accessed | tf_op | source)
XLA Modules:
  0.0 243.0 jit_solution(7660917823203948791)
XLA Ops:
  8.9 1.7 gather_fusion
  10.6 1.3 convolution_convert_fusion.4
  11.8 5.4 %all-to-all-start = ((bf16[8,2,128,128]{3,2,1,0:T(8,128)(2,1)}), bf16[8,2,128,128]{3,2,1,0:T(8,128)(2,1)S(1)}, u32[]{:S(2)}, u32[]{:S(2)}) async-start(bf16[8,2,128,128]{3,2,1,0:T(8,128)(2,1)} %bitcast.6), calls=%async_computation | async-start | bytes 1048576 | tf_op jit(solution)/shard_map/all_to_all | solution.py:98
  20.7 1.2 fusion.27
  22.0 2.0 all-to-all-done
  25.2 1.4 multiply_convert_fusion.1
  27.7 1.0 fusion.20
  28.7 1.2 convolution_convert_fusion.5
  30.7 1.2 multiply_convert_fusion
  32.0 1.0 convert_reduce_fusion.1
  33.7 1.1 convolution_convert_fusion.1
  34.8 2.5 %gather_fusion.2 = bf16[16,128,128]{2,1,0:T(8,128)(2,1)} fusion(bf16[16,128,128]{2,1,0:T(8,128)(2,1)} %bitcast.108, s32[1024]{0:T(1024)S(1)} %pad_clamp_fusion), kind=kCustom, calls=%fused_computation.2 | custom fusion | bytes 1048640 | tf_op jit(solution)/shard_map/gather | solution.py:43
  37.2 2.3 convert_reduce_fusion.2
  40.5 1.0 fusion.60
  41.5 1.0 convert_reduce_fusion.3
  44.1 1.1 convolution_convert_fusion
  47.2 1.1 fusion.11
  49.0 41.2 %all-reduce = (f32[128]{0:T(128)S(1)}, f32[128]{0:T(128)S(1)}, f32[128]{0:T(128)S(1)}, f32[128]{0:T(128)S(1)}) all-reduce(f32[128]{0:T(128)} %get-tuple-element.30, f32[128]{0:T(128)S(1)} %copy-done.27, f32[128]{0:T(128)S(1)} %copy-done.26, f32[128]{0:T(128)S(1)} %copy-done.23), channel_id=1, replica_groups=mesh['events'=4,'nodes'=8] {'events','nodes'}, use_global_device_ids=true, to_apply=%region_2.4 | all-reduce | flops 512 | bytes 4096 | tf_op jit(solution)/shard_map/psum | solution.py:177
  92.3 1.2 fusion.22
  94.2 3.4 %collective-permute-start.6 = (bf16[1,2,128,128]{3,2,1,0:T(8,128)(2,1)}, bf16[1,2,128,128]{3,2,1,0:T(8,128)(2,1)}, u32[]{:S(2)}, u32[]{:S(2)}) collective-permute-start(bf16[1,2,128,128]{3,2,1,0:T(8,128)(2,1)} %get-tuple-element.19), channel_id=1, source_target_pairs={{0,1},{1,2},{2,3},{3,4},{4,5},{5,6},{6,7},{7,0},{8,9},{9,10},{10,1... | collective-permute-start | bytes 196616 | tf_op jit(solution)/shard_map/ppermute | solution.py:18
  97.6 1.2 collective-permute-start.5
  99.4 1.5 collective-permute-start
  100.9 1.5 fusion.19
  102.5 1.2 fusion.15
  107.7 2.3 collective-permute-done.1
  110.0 2.2 collective-permute-start.2
  112.2 1.7 collective-permute-done.2
  117.7 1.0 fusion.18
  118.7 1.2 fusion.13
  120.2 1.1 fusion.10
  121.3 111.2 %all-reduce.4.cloned.1.call-done = (f32[384,128]{1,0:T(8,128)}, f32[128,128]{1,0:T(8,128)}, f32[256,128]{1,0:T(8,128)}, f32[128,128]{1,0:T(8,128)}) async-done(((f32[384,128]{1,0:T(8,128)}, f32[128,128]{1,0:T(8,128)}, f32[256,128]{1,0:T(8,128)}, f32[128,128]{1,0:T(8,128)}), (f32[384,128]{1,0:T(8,128)}, f32[128,128]{1,0:T(8,128)}, f32[256,128]{1,0:T(8,128)}, ...) | async-done | bytes 458768 | tf_op jit(solution)/shard_map/psum | solution.py:177
  232.6 1.7 broadcast_multiply_fusion
  (125 shorter events, 27.6 us)
Async XLA Ops:
  7.2 17.3 %copy-start = (bf16[1,1,8,2,128,128]{5,4,3,2,1,0:T(8,128)(2,1)S(1)}, bf16[1,1,8,2,128,128]{5,4,3,2,1,0:T(8,128)(2,1)}, u32[]{:S(2)}) copy-start(bf16[1,1,8,2,128,128]{5,4,3,2,1,0:T(8,128)(2,1)} %param.19) | copy-start | bytes 1572868
  8.9 1.7 copy-start.16
  11.8 5.4 %copy-start.1 = (bf16[1,2048,128]{2,1,0:T(8,128)(2,1)S(1)}, bf16[1,2048,128]{2,1,0:T(8,128)(2,1)}, u32[]{:S(2)}) copy-start(bf16[1,2048,128]{2,1,0:T(8,128)(2,1)} %param.18) | copy-start | bytes 1572868
  11.8 12.1 %all-to-all-start = ((bf16[8,2,128,128]{3,2,1,0:T(8,128)(2,1)}), bf16[8,2,128,128]{3,2,1,0:T(8,128)(2,1)S(1)}, u32[]{:S(2)}, u32[]{:S(2)}) async-start(bf16[8,2,128,128]{3,2,1,0:T(8,128)(2,1)} %bitcast.6), calls=%async_computation | async-start | bytes 1048576 | tf_op jit(solution)/shard_map/all_to_all | solution.py:98
  17.2 215.4 %all-reduce.4.cloned.1.call-start = ((), (), s32[]{:S(2)}) async-start(), calls=%async_computation.1 | async-start | bytes 917504 | tf_op jit(solution)/shard_map/psum | solution.py:177
  18.6 1.3 copy-start.2
  19.8 8.9 %copy-start.19 = (s32[16]{0:T(128)}, s32[16]{0:T(128)S(1)}, u32[]{:S(2)}) copy-start(s32[16]{0:T(128)S(1)} %eq.34) | copy-start | bytes 196
  19.9 0.8 copy-start.9
  20.7 3.2 %copy-start.7 = (bf16[384,128]{1,0:T(8,128)(2,1)S(1)}, bf16[384,128]{1,0:T(8,128)(2,1)}, u32[]{:S(2)}) copy-start(bf16[384,128]{1,0:T(8,128)(2,1)} %param.25) | copy-start | bytes 294916
  25.2 1.5 copy-start.28
  26.6 1.1 copy-start.5
  28.7 1.4 copy-start.4
  30.7 1.3 copy-start.17
  39.5 1.0 copy-start.6
  39.5 2.0 copy-start.32
  43.2 0.9 copy-start.8
  45.2 1.0 copy-start.3
  46.3 1.0 copy-start.18
  46.3 1.0 copy-start.25
  94.2 22.3 %collective-permute-start.6 = (bf16[1,2,128,128]{3,2,1,0:T(8,128)(2,1)}, bf16[1,2,128,128]{3,2,1,0:T(8,128)(2,1)}, u32[]{:S(2)}, u32[]{:S(2)}) collective-permute-start(bf16[1,2,128,128]{3,2,1,0:T(8,128)(2,1)} %get-tuple-element.19), channel_id=1, source_target_pairs={{0,1},{1,2},{2,3},{3,4},{4,5},{5,6},{6,7},{7,0},{8,9},{9,10},{10,1... | collective-permute-start | bytes 196616 | tf_op jit(solution)/shard_map/ppermute | solution.py:18
  97.6 18.1 %collective-permute-start.5 = (bf16[1,2,128,128]{3,2,1,0:T(8,128)(2,1)}, bf16[1,2,128,128]{3,2,1,0:T(8,128)(2,1)}, u32[]{:S(2)}, u32[]{:S(2)}) collective-permute-start(bf16[1,2,128,128]{3,2,1,0:T(8,128)(2,1)} %get-tuple-element.20), channel_id=1, source_target_pairs={{0,2},{1,3},{2,4},{3,5},{4,6},{5,7},{6,0},{7,1},{8,10},{9,11},{10,... | collective-permute-start | bytes 196616 | tf_op jit(solution)/shard_map/ppermute | solution.py:18
  98.8 16.0 %collective-permute-start.4 = (bf16[1,2,128,128]{3,2,1,0:T(8,128)(2,1)}, bf16[1,2,128,128]{3,2,1,0:T(8,128)(2,1)}, u32[]{:S(2)}, u32[]{:S(2)}) collective-permute-start(bf16[1,2,128,128]{3,2,1,0:T(8,128)(2,1)} %get-tuple-element.21), channel_id=1, source_target_pairs={{0,3},{1,4},{2,5},{3,6},{4,7},{5,0},{6,1},{7,2},{8,11},{9,12},{10,... | collective-permute-start | bytes 196616 | tf_op jit(solution)/shard_map/ppermute | solution.py:18
  98.8 15.2 %collective-permute-start.3 = (bf16[1,2,128,128]{3,2,1,0:T(8,128)(2,1)}, bf16[1,2,128,128]{3,2,1,0:T(8,128)(2,1)}, u32[]{:S(2)}, u32[]{:S(2)}) collective-permute-start(bf16[1,2,128,128]{3,2,1,0:T(8,128)(2,1)} %get-tuple-element.22), channel_id=1, source_target_pairs={{0,4},{1,5},{2,6},{3,7},{4,0},{5,1},{6,2},{7,3},{8,12},{9,13},{10,... | collective-permute-start | bytes 196616 | tf_op jit(solution)/shard_map/ppermute | solution.py:18
  99.4 6.0 %collective-permute-start = (bf16[1,2,128,128]{3,2,1,0:T(8,128)(2,1)}, bf16[1,2,128,128]{3,2,1,0:T(8,128)(2,1)}, u32[]{:S(2)}, u32[]{:S(2)}) collective-permute-start(bf16[1,2,128,128]{3,2,1,0:T(8,128)(2,1)} %get-tuple-element.25), channel_id=1, source_target_pairs={{0,7},{1,0},{2,1},{3,2},{4,3},{5,4},{6,5},{7,6},{8,15},{9,8},{10,9... | collective-permute-start | bytes 196616 | tf_op jit(solution)/shard_map/ppermute | solution.py:18
  100.9 1.5 copy-start.20
  106.2 3.7 %copy-start.12 = (bf16[1,2,128,128]{3,2,1,0:T(8,128)(2,1)S(1)}, bf16[1,2,128,128]{3,2,1,0:T(8,128)(2,1)}, u32[]{:S(2)}) copy-start(bf16[1,2,128,128]{3,2,1,0:T(8,128)(2,1)} %get-tuple-element.23) | copy-start | bytes 196612
  106.2 3.7 %collective-permute-start.1 = (bf16[1,2,128,128]{3,2,1,0:T(8,128)(2,1)S(1)}, bf16[1,2,128,128]{3,2,1,0:T(8,128)(2,1)S(1)}, u32[]{:S(2)}, u32[]{:S(2)}) collective-permute-start(bf16[1,2,128,128]{3,2,1,0:T(8,128)(2,1)S(1)} %copy-done.13), channel_id=1, source_target_pairs={{0,6},{1,7},{2,0},{3,1},{4,2},{5,3},{6,4},{7,5},{8,14},{9,15},{10,... | collective-permute-start | bytes 196616 | tf_op jit(solution)/shard_map/ppermute | solution.py:18
  110.0 4.0 %collective-permute-start.2 = (bf16[1,2,128,128]{3,2,1,0:T(8,128)(2,1)S(1)}, bf16[1,2,128,128]{3,2,1,0:T(8,128)(2,1)S(1)}, u32[]{:S(2)}, u32[]{:S(2)}) collective-permute-start(bf16[1,2,128,128]{3,2,1,0:T(8,128)(2,1)S(1)} %copy-done.12), channel_id=1, source_target_pairs={{0,5},{1,6},{2,7},{3,0},{4,1},{5,2},{6,3},{7,4},{8,13},{9,14},{10,... | collective-permute-start | bytes 196616 | tf_op jit(solution)/shard_map/ppermute | solution.py:18
  117.7 1.0 copy-start.22
  232.6 1.7 copy-start.15
  232.6 2.3 copy-start.14
  234.2 1.3 copy-start.10
  (10 other events, 6.9 us)
Sparse Core Ops, SparseCore 0:
  105.5 126.9 all-reduce.3
